TPU v7x, 32 devices: a whole 2x2x4 slice. The times are simulated.
32 devices in a mesh: tm: 4 (over y, core), space: 8 (over z, x).
Axes of the slice: x: 2, y: 2, z: 4, core: 2. Of those that a mesh axis runs over, the one named last changes fastest.
Arguments:
- background: bfloat16 [65536, 64], P('space'), may hold values from -4 to 4
- probe: bfloat16 [64, 32], replicated, may hold values from -0.75 to 0.75
- member_scale: float32 [64], replicated, may hold values from 0.5 to 2
- decay: float32 [12, 32], P('tm'), may hold values from 0.36 to 1
- inflation: float32 [12], P('tm'), may hold values from 0.05 to 0.5
- obs_owner: int32 [12, 16384, 1], P('tm', 'space'), may hold values from 0 to 7; in each aligned block of 2048 rows (0 to 2047, 2048 to 4095, ..., all dimensions but the last counted through in order) at most 512 rows name the same one
- obs_offset: int32 [12, 16384], P('tm', 'space'), may hold values from 0 to 8191
- obs_value: float32 [12, 16384], P('tm', 'space'), may hold values from -360 to 360
- obs_weight: float32 [12, 16384], P('tm', 'space'), may hold values from 0.0002 to 0.002
Outputs:
- smooth_mean: float32 [12, 65536], P('tm', 'space')
- smooth_spread: float32 [12, 65536], P('tm', 'space')
Inputs may be any that keep to these rules, and one draw needn't show every extreme that they name: `obs_owner`: of the 2048 observations that one reader holds for one day, at most 512 name the same owner, and 512 is reached.
All inputs are finite; a program needn't handle non-finite values.
Results may differ from a plain program's by a relative error of at most 0.0029.
Values sent between devices are 32-bit elements; how exact they have to be, the bound alone decides.
A program may use at most 64 MiB of HBM per device.

v0:
```python
import jax
import jax.numpy as jnp
from jax import lax
from jax.sharding import PartitionSpec as P

HIGHEST = lax.Precision.HIGHEST


def prefix(part, axis, combine, identity, reverse):
    count = lax.axis_size(axis)
    place = lax.axis_index(axis)
    ahead = count - 1 - place if reverse else place
    gathered = jax.tree.map(lambda a: lax.all_gather(a, axis), part)
    state = jax.tree.map(lambda a, e: jnp.zeros_like(a) + jnp.asarray(e, a.dtype), part, identity)

    def one(step, state):
        source = count - 1 - step if reverse else step
        return combine(
            state, jax.tree.map(lambda a: lax.dynamic_index_in_dim(a, source, 0, False), gathered)
        )

    return lax.fori_loop(0, ahead, one, state)


def passed_along(value, axis, steps):
    count = lax.axis_size(axis)
    initial, last = (max(0, -steps), min(count, count - steps))
    return lax.ppermute(value, axis, [(source, source + steps) for source in range(initial, last)])


def matmul_high(left_mat, right_mat):
    return jnp.matmul(left_mat, right_mat, precision=HIGHEST)


def matvec_high(matrix, vector):
    return matmul_high(matrix, vector[..., None])[..., 0]


def flip_last(matrix):
    return jnp.swapaxes(matrix, -1, -2)


def symmetric(matrix):
    return 0.5 * (matrix + flip_last(matrix))


def spd_solve(matrix, right_side):
    lower_chol = jnp.linalg.cholesky(matrix)
    middle = lax.linalg.triangular_solve(lower_chol, right_side, left_side=True, lower=True)
    return lax.linalg.triangular_solve(
        lower_chol, middle, left_side=True, lower=True, transpose_a=True
    )


def spd_inverse(matrix):
    identity_mat = jnp.broadcast_to(jnp.eye(matrix.shape[-1], dtype=jnp.float32), matrix.shape)
    return spd_solve(matrix, identity_mat)


def filter_combine(left_elem, right_elem):
    trans_a, mean_a, cov_a, vec_a, prec_a = left_elem
    trans_b, mean_b, cov_b, vec_b, prec_b = right_elem
    width = cov_a.shape[-1]
    coupled = jnp.eye(width, dtype=jnp.float32) + matmul_high(cov_a, prec_b)
    normal_mat = matmul_high(flip_last(coupled), coupled)
    coupled_inv = spd_solve(normal_mat, flip_last(coupled))
    left_gain = matmul_high(trans_b, coupled_inv)
    transition = matmul_high(left_gain, trans_a)
    mean_out = matvec_high(left_gain, mean_a + matvec_high(cov_a, vec_b)) + mean_b
    cov_out = symmetric(matmul_high(matmul_high(left_gain, cov_a), flip_last(trans_b)) + cov_b)
    back_gain = matmul_high(flip_last(trans_a), flip_last(coupled_inv))
    vec_out = matvec_high(back_gain, vec_b - matvec_high(prec_b, mean_a)) + vec_a
    prec_out = symmetric(matmul_high(matmul_high(back_gain, prec_b), trans_a) + prec_a)
    return (transition, mean_out, cov_out, vec_out, prec_out)


def smooth_combine(left_elem, right_elem):
    gain_a, mean_a, cov_a = left_elem
    gain_b, mean_b, cov_b = right_elem
    gain_out = matmul_high(gain_a, gain_b)
    mean_out = matvec_high(gain_a, mean_b) + mean_a
    cov_out = symmetric(matmul_high(matmul_high(gain_a, cov_b), flip_last(gain_a)) + cov_a)
    return (gain_out, mean_out, cov_out)


def make_reader(rows_source, received):
    values = received[0]
    weights = received[1]
    offsets = received[2].astype(jnp.int32)
    basis_rows = rows_source[offsets]
    weighted = basis_rows * weights[..., None]
    core_part = jnp.einsum("sdcr,sdcq->drq", weighted, basis_rows, precision=HIGHEST)
    vector_part = jnp.einsum("sdcr,sdc->dr", weighted, values, precision=HIGHEST)
    return (core_part, vector_part)


def subspace_setup(member_gram, probe_wide, field_basis, member_scale):
    mode_count = probe_wide.shape[1]
    core_gram = matmul_high(matmul_high(probe_wide.T, member_gram), probe_wide)
    lower_chol = jnp.linalg.cholesky(core_gram)
    lower_inv = lax.linalg.triangular_solve(
        lower_chol, jnp.eye(mode_count, dtype=jnp.float32), left_side=True, lower=True
    )
    basis = matmul_high(field_basis, lower_inv.T)
    projected = matmul_high(lower_inv, matmul_high(probe_wide.T, member_gram))
    prior_cov = matmul_high(projected * (member_scale * member_scale)[None, :], projected.T)
    return (lower_inv, basis, prior_cov)


def body(
    background, probe, member_scale, decay, inflation, obs_owner, obs_offset, obs_value, obs_weight
):
    mode_count = probe.shape[1]
    days_dev = decay.shape[0]
    obs_dev = obs_offset.shape[1]
    space_count = lax.axis_size("space")
    time_count = lax.axis_size("tm")
    time_index = lax.axis_index("tm")
    bucket_cap = 2 * obs_dev // space_count
    identity_mat = jnp.eye(mode_count, dtype=jnp.float32)
    zero_mat = jnp.zeros((mode_count, mode_count), jnp.float32)
    zero_vec = jnp.zeros((mode_count,), jnp.float32)
    scaled_probe = (probe.astype(jnp.float32) * member_scale[:, None]).astype(jnp.bfloat16)
    probe_wide = scaled_probe.astype(jnp.float32)
    field_basis = jnp.dot(background, scaled_probe, preferred_element_type=jnp.float32)
    local_gram = jnp.dot(background.T, background, preferred_element_type=jnp.float32)
    owners = obs_owner[:, :, 0]
    owner_hits = (
        owners[:, :, None] == jnp.arange(space_count, dtype=jnp.int32)[None, None, :]
    ).astype(jnp.int32)
    earlier_hits = jnp.cumsum(owner_hits, axis=1) - owner_hits
    slot_index = jnp.sum(earlier_hits * owner_hits, axis=2)
    day_index = jnp.broadcast_to(jnp.arange(days_dev, dtype=jnp.int32)[:, None], owners.shape)
    packed = jnp.stack([obs_value, obs_weight, obs_offset.astype(jnp.float32)], axis=0)
    buckets = (
        jnp.zeros((3, space_count, days_dev, bucket_cap), jnp.float32)
        .at[:, owners, day_index, slot_index]
        .set(packed)
    )
    core_field, vector_field = make_reader(
        field_basis, lax.all_to_all(buckets, "space", split_axis=1, concat_axis=1, tiled=True)
    )
    member_gram, core_field, vector_field = lax.psum(
        (local_gram, core_field, vector_field), "space"
    )
    lower_inv, basis, prior_cov = subspace_setup(member_gram, probe_wide, field_basis, member_scale)
    precision_core = matmul_high(matmul_high(lower_inv, core_field), lower_inv.T)
    info_vector = matmul_high(vector_field, lower_inv.T)
    noise_cov = inflation[:, None, None] * prior_cov
    noise_inv = spd_inverse(noise_cov)
    elem_cov = symmetric(spd_inverse(noise_inv + precision_core))
    elem_trans = matmul_high(elem_cov, noise_inv) * decay[:, None, :]
    elem_mean = matvec_high(elem_cov, info_vector)
    corrected = precision_core - matmul_high(matmul_high(precision_core, elem_cov), precision_core)
    elem_prec = decay[:, :, None] * corrected * decay[:, None, :]
    elem_vec = decay * (info_vector - matvec_high(precision_core, elem_mean))
    elements = (elem_trans, elem_mean, elem_cov, elem_vec, elem_prec)
    prior_elem = (zero_mat, zero_vec, prior_cov, zero_vec, zero_mat)
    first_elem = tuple((member[0] for member in elements))
    merged = filter_combine(prior_elem, first_elem)
    is_opening_day = time_index == 0
    elements = tuple(
        (
            member.at[0].set(jnp.where(is_opening_day, joined, member[0]))
            for member, joined in zip(elements, merged)
        )
    )
    local_prefix = lax.associative_scan(filter_combine, elements)
    total_trans, total_mean, total_cov, total_vec, total_prec = tuple(
        (member[-1] for member in local_prefix)
    )
    filter_identity = (identity_mat, zero_vec, zero_mat, zero_vec, zero_mat)
    from_left = prefix(
        (total_trans, total_mean, total_cov, total_vec, total_prec),
        "tm",
        filter_combine,
        filter_identity,
        False,
    )
    filtered = filter_combine(from_left, local_prefix)
    filt_mean = filtered[1]
    filtered_covariance = filtered[2]
    next_decay, next_infl = passed_along((decay[0:1], inflation[0:1]), "tm", -1)
    decay_next = jnp.concatenate([decay[1:], next_decay], axis=0)
    infl_next = jnp.concatenate([inflation[1:], next_infl], axis=0)
    day_pos = jnp.arange(days_dev, dtype=jnp.int32)
    is_last = jnp.logical_and(time_index == time_count - 1, day_pos == days_dev - 1)
    infl_next = jnp.where(is_last, 1.0, infl_next)
    predicted = (
        decay_next[:, :, None] * filtered_covariance * decay_next[:, None, :]
        + infl_next[:, None, None] * prior_cov
    )
    rescaled_covariance = decay_next[:, :, None] * filtered_covariance
    gain_days = flip_last(spd_solve(predicted, rescaled_covariance))
    shifted_mean = filt_mean - matvec_high(gain_days, decay_next * filt_mean)
    resid_cov = symmetric(filtered_covariance - matmul_high(gain_days, rescaled_covariance))
    gain_days = jnp.where(is_last[:, None, None], 0.0, gain_days)
    shifted_mean = jnp.where(is_last[:, None], filt_mean, shifted_mean)
    resid_cov = jnp.where(is_last[:, None, None], filtered_covariance, resid_cov)

    def reverse_local(after_part, before_part):
        return smooth_combine(before_part, after_part)

    local_suffix = lax.associative_scan(
        reverse_local, (gain_days, shifted_mean, resid_cov), reverse=True
    )
    head_gain, head_mean, head_cov = tuple((member[0] for member in local_suffix))
    smooth_identity = (identity_mat, zero_vec, zero_mat)
    from_right = prefix(
        (head_gain, head_mean, head_cov), "tm", reverse_local, smooth_identity, True
    )
    smoothed = smooth_combine(local_suffix, from_right)
    sm_mean = smoothed[1]
    sm_cov = smoothed[2]
    smooth_mean = matmul_high(sm_mean, basis.T)

    def spread_day(cov_day):
        return jnp.sum(matmul_high(basis, cov_day) * basis, axis=1)

    smooth_spread = lax.map(spread_day, sm_cov)
    return (smooth_mean, smooth_spread)


def solution(mesh):
    return jax.shard_map(
        body,
        mesh=mesh,
        in_specs=(
            P("space", None),
            P(),
            P(),
            P("tm", None),
            P("tm"),
            P("tm", "space", None),
            P("tm", "space"),
            P("tm", "space"),
            P("tm", "space"),
        ),
        out_specs=(P("tm", "space"), P("tm", "space")),
        check_vma=False,
    )
```

profile of v0, /device:TPU:0, one launch (start us, length us, event | category | flops | bytes accessed | tf_op | source)
XLA Modules:
  0.0 341.7 jit_solution(8476068816161385312)
XLA Ops:
  2.2 6.8 %reduce-window.6 = s32[3,8,16,128]{3,2,1,0:T(8,128)S(1)} reduce-window(s32[3,8,16,128]{3,2,1,0:T(8,128)S(1)} %fusion.82, s32[]{:T(128)} %constant.321.clone.1), window={size=1x1x1x128 pad=0_0x0_0x0_0x127_0}, to_apply=%region_5.11 | reduce-window | flops 6242304 | bytes 393220 | tf_op jit(solution)/shard_map/reduce-window
  16.7 18.9 %scatter_custom_fusion = f32[3,12288]{0,1:T(8,128)} fusion(s32[6144]{0:T(1024)S(1)} %reshape.541, f32[6144,3]{1,0:T(8,128)} %bitcast.798, f32[]{:T(128)} %constant.320.clone.1), kind=kCustom, calls=%fused_computation.69 | custom fusion | bytes 147968
  35.6 5.6 %copy.207 = f32[3,3,8,512]{3,1,0,2:T(4,128)} copy(f32[3,3,8,512]{0,3,2,1:T(8,128)} %bitcast.795) | data formatting | bytes 294912
  41.2 7.3 %all-to-all-start = ((f32[3,8,3,512]{3,2,0,1:T(4,128)}), f32[3,8,3,512]{3,2,0,1:T(4,128)S(1)}, u32[]{:S(2)}, u32[]{:S(2)}) async-start(f32[3,8,3,512]{3,2,0,1:T(4,128)} %bitcast.44), calls=%async_computation | async-start | bytes 393216 | tf_op jit(solution)/shard_map/all_to_all | solution.py:141
  52.0 2.7 copy.210
  56.6 43.2 %gather_fusion = f32[12288,32]{1,0:T(8,128)} fusion(f32[8192,32]{1,0:T(8,128)} %copy.210, s32[12288]{0:T(1024)S(1)} %broadcast_clamp_fusion), kind=kCustom, calls=%fused_computation | custom fusion | bytes 3194880 | tf_op jit(solution)/shard_map/gather | solution.py:90
  99.8 4.3 %copy.213 = f32[8,3,512,32]{2,3,1,0:T(8,128)S(1)} copy(f32[8,3,512,32]{3,2,1,0:T(8,128)} %bitcast.793) | data formatting | bytes 3145728 | tf_op jit(solution)/shard_map/gather | solution.py:90
  104.3 5.5 %fusion.55 = f32[3,32,32]{2,1,0:T(8,128)S(1)} fusion(f32[8,3,512,32]{3,2,1,0:T(8,128)} %bitcast.794, f32[8,3,512,32]{2,3,1,0:T(8,128)S(1)} %copy.213, f32[8,3,512]{2,1,0:T(4,128)S(1)} %copy.212), kind=kOutput, calls=%fused_computation.78 | convolution fusion | flops 151388160 | bytes 3207168 | tf_op jit(solution)/shard_map/sdcr,sdcq->drq/dot_general | solution.py:92
  111.2 37.8 %all-reduce.16 = (f32[64,64]{1,0:T(8,128)S(1)}, f32[3,32,32]{2,1,0:T(8,128)S(1)}, f32[3,32]{1,0:T(4,128)S(1)}) all-reduce(f32[64,64]{1,0:T(8,128)S(1)} %fusion.280, f32[3,32,32]{2,1,0:T(8,128)S(1)} %fusion.55, f32[3,32]{1,0:T(4,128)S(1)} %bitcast.827), channel_id=1, replica_groups=mesh['tm'=4,'space'=8] {'space'}, use_global_device_ids=true, to_apply=%region_0.0 | all-reduce | flops 7264 | bytes 58112 | tf_op jit(solution)/shard_map/psum | solution.py:143
  149.4 2.9 custom-call.47
  153.6 2.4 custom-call.48
  156.9 8.8 %custom-call.49 = f32[3,32,32]{2,1,0:T(8,128)S(1)} custom-call(f32[3,32,32]{2,1,0:T(8,128)S(1)} %fusion.110), custom_call_target="Cholesky" | custom-call | tf_op jit(solution)/shard_map/jit(cholesky)/cholesky | solution.py:48
  165.9 7.4 %custom-call.51 = f32[3,1,32,32]{2,3,1,0:T(8,128)S(1)} custom-call(f32[3,1,32,32]{3,2,1,0:T(8,128)S(1)} %select_bitcast_fusion.3), custom_call_target="InvertDiagBlocksLowerTriangular" | custom-call | tf_op jit(solution)/shard_map/triangular_solve/custom-call.6 | solution.py:50
  174.5 8.8 %custom-call.52 = f32[3,32,32]{2,1,0:T(8,128)S(1)} custom-call(f32[3,32,32]{2,1,0:T(8,128)S(1)} %fusion.105), custom_call_target="Cholesky" | custom-call | tf_op jit(solution)/shard_map/jit(cholesky)/cholesky | solution.py:48
  183.5 7.4 %custom-call.54 = f32[3,1,32,32]{2,3,1,0:T(8,128)S(1)} custom-call(f32[3,1,32,32]{3,2,1,0:T(8,128)S(1)} %select_bitcast_fusion.2), custom_call_target="InvertDiagBlocksLowerTriangular" | custom-call | tf_op jit(solution)/shard_map/triangular_solve/custom-call.6 | solution.py:50
  192.6 2.9 custom-call.55
  200.8 2.9 custom-call.58
  205.0 2.4 custom-call.60
  211.4 2.9 custom-call.61
  219.6 6.6 %all_gather.28 = f32[4,32,32]{2,1,0:T(8,128)S(1)} all-gather(f32[1,32,32]{2,1,0:T(8,128)S(1)} %copy.242), channel_id=1, replica_groups=mesh['tm'=4,'space'=8] {'tm'}, dimensions={0}, use_global_device_ids=true | all-gather | bytes 20480 | tf_op jit(solution)/shard_map/all_gather | solution.py:13
  226.3 5.3 %all-gather.1 = f32[4,1,32]{2,1,0:T(1,128)S(1)} all-gather(f32[1,1,32]{2,1,0:T(1,128)S(1)} %slice_bitcast_fusion.16), channel_id=1, replica_groups=mesh['tm'=4,'space'=8] {'tm'}, dimensions={0}, use_global_device_ids=true | all-gather | bytes 640 | tf_op jit(solution)/shard_map/all_gather | solution.py:13
  232.6 5.0 %all-gather = f32[4,1,32]{2,1,0:T(1,128)S(1)} all-gather(f32[1,1,32]{2,1,0:T(1,128)S(1)} %slice_bitcast_fusion.17), channel_id=1, replica_groups=mesh['tm'=4,'space'=8] {'tm'}, dimensions={0}, use_global_device_ids=true | all-gather | bytes 640 | tf_op jit(solution)/shard_map/all_gather | solution.py:13
  238.6 5.2 %all_gather.25 = f32[4,32,32]{2,1,0:T(8,128)S(1)} all-gather(f32[1,32,32]{2,1,0:T(8,128)S(1)} %copy.237), channel_id=1, replica_groups=mesh['tm'=4,'space'=8] {'tm'}, dimensions={0}, use_global_device_ids=true | all-gather | bytes 20480 | tf_op jit(solution)/shard_map/all_gather | solution.py:13
  243.9 5.2 %all_gather.24 = f32[4,32,32]{2,1,0:T(8,128)S(1)} all-gather(f32[1,32,32]{2,1,0:T(8,128)S(1)} %fusion.139), channel_id=1, replica_groups=mesh['tm'=4,'space'=8] {'tm'}, dimensions={0}, use_global_device_ids=true | all-gather | bytes 20480 | tf_op jit(solution)/shard_map/all_gather | solution.py:13
  250.0 8.8 %custom-call.64 = f32[3,32,32]{2,1,0:T(8,128)S(1)} custom-call(f32[3,32,32]{2,1,0:T(8,128)S(1)} %fusion.97), custom_call_target="Cholesky" | custom-call | tf_op jit(solution)/shard_map/jit(cholesky)/cholesky | solution.py:48
  259.0 7.4 %custom-call.66 = f32[3,1,32,32]{2,3,1,0:T(8,128)S(1)} custom-call(f32[3,1,32,32]{3,2,1,0:T(8,128)S(1)} %select_bitcast_fusion.1), custom_call_target="InvertDiagBlocksLowerTriangular" | custom-call | tf_op jit(solution)/shard_map/triangular_solve/custom-call.6 | solution.py:50
  268.1 8.8 %custom-call.67 = f32[3,32,32]{2,1,0:T(8,128)S(1)} custom-call(f32[3,32,32]{2,1,0:T(8,128)S(1)} %fusion.92), custom_call_target="Cholesky" | custom-call | tf_op jit(solution)/shard_map/jit(cholesky)/cholesky | solution.py:48
  277.1 7.4 %custom-call.69 = f32[3,1,32,32]{2,3,1,0:T(8,128)S(1)} custom-call(f32[3,1,32,32]{3,2,1,0:T(8,128)S(1)} %select_bitcast_fusion), custom_call_target="InvertDiagBlocksLowerTriangular" | custom-call | tf_op jit(solution)/shard_map/triangular_solve/custom-call.6 | solution.py:50
  288.6 30.8 %all_gather.31 = f32[4,32,32]{2,1,0:T(8,128)S(1)} all-gather(f32[1,32,32]{2,1,0:T(8,128)S(1)} %copy.265), channel_id=1, replica_groups=mesh['tm'=4,'space'=8] {'tm'}, dimensions={0}, use_global_device_ids=true | all-gather | bytes 20480 | tf_op jit(solution)/shard_map/all_gather | solution.py:13
  319.4 5.2 %all_gather.29 = f32[4,32,32]{2,1,0:T(8,128)S(1)} all-gather(f32[1,32,32]{2,1,0:T(8,128)S(1)} %fusion.142), channel_id=1, replica_groups=mesh['tm'=4,'space'=8] {'tm'}, dimensions={0}, use_global_device_ids=true | all-gather | bytes 20480 | tf_op jit(solution)/shard_map/all_gather | solution.py:13
  324.6 5.0 %all-gather.2 = f32[4,1,32]{2,1,0:T(1,128)S(1)} all-gather(f32[1,1,32]{2,1,0:T(1,128)S(1)} %slice_bitcast_fusion.15), channel_id=1, replica_groups=mesh['tm'=4,'space'=8] {'tm'}, dimensions={0}, use_global_device_ids=true | all-gather | bytes 640 | tf_op jit(solution)/shard_map/all_gather | solution.py:13
  331.9 8.3 %while.49 = (s32[]{:T(128)}, f32[3,8192]{1,0:T(4,128)}, f32[3,32,32]{1,2,0:T(8,128)S(1)}, f32[8192,32]{0,1:T(8,128)S(1)}, s32[]{:T(128)}, /*index=5*/s32[]{:T(128)}) while((s32[]{:T(128)}, f32[3,8192]{1,0:T(4,128)}, f32[3,32,32]{1,2,0:T(8,128)S(1)}, f32[8192,32]{0,1:T(8,128)S(1)}, s32[]{:T(128)}, /*index=5*/s32[]{:T(128)}) %tuple.118), condition=%wide.region_19.29_spmd, body=%wide.region_17.28_spmd.sunk | while | flops 101179392 | bytes 2211917 | solution.py:220
  (298 shorter events, 59.7 us)
Async XLA Ops:
  0.6 50.5 %copy-start = (bf16[8192,64]{0,1:T(8,128)(2,1)S(1)}, bf16[8192,64]{0,1:T(8,128)(2,1)}, u32[]{:S(2)}) copy-start(bf16[8192,64]{0,1:T(8,128)(2,1)} %param.40) | copy-start | bytes 3145732
  35.6 12.9 %copy-start.4 = (f32[3,32]{1,0:T(4,128)S(1)}, f32[3,32]{1,0:T(4,128)}, u32[]{:S(2)}) copy-start(f32[3,32]{1,0:T(4,128)} %param.43) | copy-start | bytes 1156
  35.6 14.2 %copy-start.6 = (f32[3]{0:T(128)S(1)}, f32[3]{0:T(128)}, u32[]{:S(2)}) copy-start(f32[3]{0:T(128)} %param.44) | copy-start | bytes 40
  35.6 16.0 %copy-start.3 = (bf16[64,32]{0,1:T(8,128)(2,1)S(1)}, bf16[64,32]{0,1:T(8,128)(2,1)}, u32[]{:S(2)}) copy-start(bf16[64,32]{0,1:T(8,128)(2,1)} %param.41) | copy-start | bytes 12292
  35.6 16.0 %copy-start.5 = (f32[64]{0:T(128)S(1)}, f32[64]{0:T(128)}, u32[]{:S(2)}) copy-start(f32[64]{0:T(128)} %param.42) | copy-start | bytes 772
  41.2 15.2 %all-to-all-start = ((f32[3,8,3,512]{3,2,0,1:T(4,128)}), f32[3,8,3,512]{3,2,0,1:T(4,128)S(1)}, u32[]{:S(2)}, u32[]{:S(2)}) async-start(f32[3,8,3,512]{3,2,0,1:T(4,128)} %bitcast.44), calls=%async_computation | async-start | bytes 393216 | tf_op jit(solution)/shard_map/all_to_all | solution.py:141
  48.5 219.3 %collective-permute-start = (f32[1,32]{1,0:T(1,128)S(1)}, f32[1,32]{1,0:T(1,128)S(1)}, u32[]{:S(2)}, u32[]{:S(2)}) collective-permute-start(f32[1,32]{1,0:T(1,128)S(1)} %slice.333), channel_id=1, source_target_pairs={{8,0},{16,8},{24,16},{9,1},{17,9},{25,17},{10,2},{18,10},{26,18},{... | collective-permute-start | bytes 392 | tf_op jit(solution)/shard_map/ppermute | solution.py:28
  49.8 5.0 %collective-permute-start.1 = (f32[1]{0:T(128)S(1)}, f32[1]{0:T(128)}, u32[]{:S(2)}, u32[]{:S(2)}) collective-permute-start(f32[1]{0:T(128)S(1)} %bitcast.830), channel_id=1, source_target_pairs={{8,0},{16,8},{24,16},{9,1},{17,9},{25,17},{10,2},{18,10},{26,18},{... | collective-permute-start | bytes 20 | tf_op jit(solution)/shard_map/ppermute | solution.py:28
  51.9 47.9 %copy-start.1 = (f32[32,8192]{1,0:T(8,128)}, f32[32,8192]{1,0:T(8,128)S(1)}, u32[]{:S(2)}) copy-start(f32[32,8192]{1,0:T(8,128)S(1)} %fusion.239) | copy-start | bytes 3145732
  249.2 38.1 %copy-start.2 = (f32[32,8192]{1,0:T(8,128)S(1)}, f32[32,8192]{1,0:T(8,128)}, u32[]{:S(2)}) copy-start(f32[32,8192]{1,0:T(8,128)} %copy-done.1) | copy-start | bytes 3145732
where the time goes:
time: 343 us; the launch traced here: 342 us
  other arithmetic  106 us (31%)
  blocking collectives  106 us (31%)
  local copies, waits for them, and re-layouts  86.9 us (25%)
  matrix products  29.5 us (9%)
  starting transfers between devices  9.84 us (3%)
    all_gather x8, blocking collectives, prefix(): gathered = jax.tree.map(lambda a: lax.all_gather(a, axis), part)  68.5 us
    gather x2, local copies, waits for them, and re-layouts, make_reader(): basis_rows = rows_source[offsets]  47.6 us
    another operation x22, other arithmetic, spd_solve(): lower_chol = jnp.linalg.cholesky(matrix)  46.7 us
    another operation x15, other arithmetic, spd_solve(): lax.linalg.triangular_solve(lower_chol, middle, left_side=True, lower=Tru...  39 us
    psum x1, blocking collectives, body(): lax.psum((local_gram, core_field, vector_field), 'space')  37.8 us
    unnamed x26, local copies, waits for them, and re-layouts  25.7 us
    dot_general x85, matrix products, matmul_high(): return jnp.matmul(left_mat, right_mat, precision=HIGHEST)  18.6 us
    another operation x3, other arithmetic  7.46 us
  transfers between devices with their start and end apart: 3, of which 2 were waited for; matrix products, arithmetic and copies ran while one was open for 44% of the time, Pallas kernels for 0%

commit v1 on v0

v1 whole, which is shorter than its diff:
```python
import functools

import jax
import jax.numpy as jnp
from jax import lax
from jax.experimental import pallas as pl
from jax.experimental.pallas import tpu as pltpu
from jax.sharding import PartitionSpec as P

HIGHEST = lax.Precision.HIGHEST
MESH = pl.DeviceIdType.MESH
F32 = jnp.float32
BF16 = jnp.bfloat16
LANES = 128
NT = (((1,), (1,)), ((), ()))
NN = (((1,), (0,)), ((), ()))
TN = (((0,), (0,)), ((), ()))


def dot_high(left, right, dims=NN):
    return lax.dot_general(left, right, dims, precision=HIGHEST, preferred_element_type=F32)


def dot_16(left, right, dims=NN):
    return lax.dot_general(left, right, dims, preferred_element_type=F32)


def terms(value, count):
    parts = []
    rest = value
    for step in range(count):
        part = rest.astype(BF16)
        parts.append(part)
        if step < count - 1:
            rest = rest - part.astype(F32)
    return parts


def dot_terms_tn(left, right):
    l1, l2, l3 = terms(left, 3)
    r1, r2, r3 = terms(right, 3)
    return dot_16(
        jnp.concatenate([l1, l1, l2, l2, l1, l3], axis=0),
        jnp.concatenate([r1, r2, r1, r2, r3, r1], axis=0),
        TN,
    )


def bucket_kernel(space_count, cap, owner_ref, offset_ref, value_ref, weight_ref, out_ref):
    days, count = owner_ref.shape
    chunks = count // LANES
    rows_owner = cap // LANES
    slot_rows = space_count * rows_owner
    before = lax.broadcasted_iota(jnp.int32, (LANES, LANES), 0)
    after = lax.broadcasted_iota(jnp.int32, (LANES, LANES), 1)
    earlier = (before < after).astype(F32).astype(BF16)
    ones = jnp.ones((LANES, LANES), BF16)
    owner_row = lax.broadcasted_iota(jnp.int32, (space_count, LANES), 0)
    for day in range(days):
        hits = []
        for chunk in range(chunks):
            own = owner_ref[day : day + 1, chunk * LANES : (chunk + 1) * LANES]
            hits.append((owner_row == own).astype(F32))
        stacked = jnp.concatenate(hits, axis=0).astype(BF16)
        inside = dot_16(stacked, earlier)
        totals = dot_16(stacked, ones)
        base = jnp.zeros((space_count, LANES), F32)
        slots = []
        owner_start = (owner_row * cap).astype(F32)
        for chunk in range(chunks):
            part = slice(chunk * space_count, (chunk + 1) * space_count)
            place = hits[chunk] * (inside[part] + base + owner_start)
            slots.append(jnp.sum(place, axis=0, keepdims=True))
            base = base + totals[part]
        slot = jnp.concatenate(slots, axis=1).astype(jnp.int32)
        slot_high = slot // LANES
        slot_low = slot - slot_high * LANES
        offset = offset_ref[day : day + 1, :]
        offset_high = offset // LANES
        pieces = terms(weight_ref[day : day + 1, :], 3) + terms(value_ref[day : day + 1, :], 3)
        pieces = [piece.astype(F32) for piece in pieces]
        pieces += [offset_high.astype(F32), (offset - offset_high * LANES).astype(F32)]
        in_row = lax.broadcasted_iota(jnp.int32, (slot_rows, count), 0) == slot_high
        left = jnp.concatenate(
            [jnp.where(in_row, piece, 0.0).astype(BF16) for piece in pieces], axis=0
        )
        right = (
            (lax.broadcasted_iota(jnp.int32, (LANES, count), 0) == slot_low)
            .astype(F32)
            .astype(BF16)
        )
        placed = dot_16(left, right, NT)
        cut = [placed[i * slot_rows : (i + 1) * slot_rows] for i in range(8)]
        whole = (cut[0] + cut[1] + cut[2], cut[3] + cut[4] + cut[5], cut[6] * LANES + cut[7])
        for kind in range(3):
            start = (kind * days + day) * rows_owner
            for owner in range(space_count):
                out_ref[owner, start : start + rows_owner, :] = whole[kind][
                    owner * rows_owner : (owner + 1) * rows_owner
                ]


def greet(peers_of, count):
    barrier = pltpu.get_barrier_semaphore()

    def signal(step, _):
        pl.semaphore_signal(barrier, inc=1, device_id=peers_of(step), device_id_type=MESH)
        return _

    lax.fori_loop(1, count, signal, 0)
    pl.semaphore_wait(barrier, count - 1)


def exchange_kernel(space_count, in_ref, out_ref, send_sem, recv_sem, own_sem):
    time_index = lax.axis_index("tm")
    me = lax.axis_index("space")

    def peer(step):
        return lax.rem(me + step, space_count)

    greet(lambda step: (time_index, peer(step)), space_count)

    def copy(step):
        return pltpu.make_async_remote_copy(
            src_ref=in_ref.at[peer(step)],
            dst_ref=out_ref.at[me],
            send_sem=send_sem.at[step],
            recv_sem=recv_sem.at[step],
            device_id=(time_index, peer(step)),
            device_id_type=MESH,
        )

    own = pltpu.make_async_copy(in_ref.at[me], out_ref.at[me], own_sem)
    for step in range(1, space_count):
        copy(step).start()
    own.start()
    own.wait()
    for step in range(1, space_count):
        copy(step).wait()


def sum_kernel(
    time_count, space_count, in_ref, out_ref, held, total, send_sem, recv_sem, send_all, recv_all
):
    time_index = lax.axis_index("tm")
    me = lax.axis_index("space")
    device_count = time_count * space_count

    def peer(step):
        return lax.rem(me + step, space_count)

    def any_peer(step):
        time_peer = lax.rem(time_index + step // space_count, time_count)
        return (time_peer, lax.rem(me + lax.rem(step, space_count), space_count))

    greet(any_peer, device_count)

    def copy(step):
        return pltpu.make_async_remote_copy(
            src_ref=in_ref.at[peer(step)],
            dst_ref=held.at[step],
            send_sem=send_sem.at[step],
            recv_sem=recv_sem.at[step],
            device_id=(time_index, peer(step)),
            device_id_type=MESH,
        )

    for step in range(1, space_count):
        copy(step).start()
    added = in_ref[me]
    for step in range(1, space_count):
        copy(step).wait()
        added = added + held[step]
    total[...] = added
    out_ref[time_index, me] = added

    def share(step):
        return pltpu.make_async_remote_copy(
            src_ref=total,
            dst_ref=out_ref.at[time_index, me],
            send_sem=send_all.at[step],
            recv_sem=recv_all.at[step],
            device_id=any_peer(step),
            device_id_type=MESH,
        )

    def start(step, _):
        share(step).start()
        return _

    def wait(step, _):
        share(step).wait()
        return _

    lax.fori_loop(1, device_count, start, 0)
    lax.fori_loop(1, device_count, wait, 0)


def info_kernel(days, rows_owner, got_ref, back_ref, probe_ref, extra_ref, out_ref, weighted):
    readers = got_ref.shape[0]
    members, cells = back_ref.shape
    rank = probe_ref.shape[0]
    high_count = cells // LANES
    step_rows = 8
    slots = step_rows * LANES
    high_row = lax.broadcasted_iota(jnp.int32, (high_count, slots), 0)
    low_row = lax.broadcasted_iota(jnp.int32, (LANES, slots), 0)
    weight_maps = []
    value_maps = []
    for day in range(days):
        hist = jnp.zeros((4 * high_count, LANES), F32)
        places = [(r, j) for r in range(readers) for j in range(rows_owner)]
        for first in range(0, len(places), step_rows):
            group = places[first : first + step_rows]

            def rows(kind):
                start = (kind * days + day) * rows_owner
                return jnp.concatenate(
                    [got_ref[r, start + j : start + j + 1, :] for r, j in group], axis=1
                )

            weight = rows(0)
            product = weight * rows(1)
            offset = rows(2).astype(jnp.int32)
            high = offset // LANES
            low = offset - high * LANES
            pieces = terms(weight, 2) + terms(product, 2)
            in_row = high_row == high
            left = jnp.concatenate(
                [jnp.where(in_row, piece.astype(F32), 0.0).astype(BF16) for piece in pieces],
                axis=0,
            )
            right = (low_row == low).astype(F32).astype(BF16)
            hist = hist + dot_16(left, right, NT)
        weight_maps.append(hist[:high_count] + hist[high_count : 2 * high_count])
        value_maps.append(hist[2 * high_count : 3 * high_count] + hist[3 * high_count :])

    chunk_rows = 8
    width = chunk_rows * LANES
    vec_row = lax.broadcasted_iota(jnp.int32, (16, width), 0)
    depth = (2 * days + 1) * members + 16
    sums = jnp.zeros((depth, members), F32)
    for first in range(0, high_count, chunk_rows):
        back = back_ref[:, first * LANES : first * LANES + width]
        back_wide = back.astype(F32)
        vectors = jnp.zeros((16, width), F32)
        for day in range(days):
            line = jnp.concatenate(
                [weight_maps[day][j : j + 1] for j in range(first, first + chunk_rows)], axis=1
            )
            part_high, part_low = terms(back_wide * line, 2)
            weighted[2 * day * members : (2 * day + 1) * members, :] = part_high
            weighted[(2 * day + 1) * members : (2 * day + 2) * members, :] = part_low
            line = jnp.concatenate(
                [value_maps[day][j : j + 1] for j in range(first, first + chunk_rows)], axis=1
            )
            line_high, line_low = terms(line, 2)
            vectors = jnp.where(vec_row == day, line_high.astype(F32), vectors)
            vectors = jnp.where(vec_row == day + 8, line_low.astype(F32), vectors)
        weighted[2 * days * members : (2 * days + 1) * members, :] = back
        weighted[(2 * days + 1) * members :, :] = vectors.astype(BF16)
        sums = sums + dot_16(weighted[...], back, NT)

    probe = probe_ref[...]
    columns = []
    for day in range(days):
        info = sums[2 * day * members : (2 * day + 1) * members]
        info = info + sums[(2 * day + 1) * members : (2 * day + 2) * members]
        columns.append(dot_high(dot_high(probe, info), probe, NT))
    gram = sums[2 * days * members : (2 * days + 1) * members]
    tail = sums[(2 * days + 1) * members :]
    vector_rows = tail[:8] + tail[8:]
    side = LANES - days * rank
    vector_rows = jnp.concatenate([vector_rows, jnp.zeros((side - 8, members), F32)], axis=0)
    columns.append(dot_high(probe, vector_rows, NT) + extra_ref[...])
    out_ref[:rank, :] = jnp.concatenate(columns, axis=1)
    out_ref[rank:, :] = jnp.concatenate([gram[:rank], gram[rank:]], axis=1)


def eliminate(mats, rank, only_below):
    row = lax.broadcasted_iota(jnp.int32, (rank, LANES), 0)
    mats = list(mats)
    for k in range(rank):
        for i, mat in enumerate(mats):
            col = mat[:, rank + k : rank + k + 1]
            scaled = mat[k : k + 1, :] * (1.0 / col[k : k + 1, :])
            if only_below:
                mats[i] = mat - jnp.where(row > k, col, 0.0) * scaled
            else:
                mats[i] = jnp.where(row == k, scaled, mat - col * scaled)
    return mats


def factor_rows(mat, rank, eye):
    pivots = jnp.sum(mat[:, rank : 2 * rank] * eye, axis=1, keepdims=True)
    return mat * lax.rsqrt(pivots)


def smooth_kernel(
    days_dev, pay_ref, probe_ref, scale_ref, back_ref, mean_ref, spread_ref, aug_ref, low_ref, top_ref
):
    time_count = pay_ref.shape[0]
    rank, members = probe_ref.shape
    cells = back_ref.shape[1]
    days = time_count * days_dev
    stages = (days - 1).bit_length()
    reach = 1 << (stages - 1)
    rows = lax.broadcasted_iota(jnp.int32, (rank, rank), 0)
    eye = (rows == lax.broadcasted_iota(jnp.int32, (rank, rank), 1)).astype(F32)
    zero = jnp.zeros((rank, rank), F32)
    probe = probe_ref[...]
    gram_pair = pay_ref[0, rank:, :]
    gram = jnp.concatenate([gram_pair[:, :members], gram_pair[:, members:]], axis=0)
    half = dot_high(probe, gram)
    core_gram = dot_high(half, probe, NT)
    reduced = eliminate([jnp.concatenate([zero, core_gram, eye, zero], axis=1)], rank, True)[0]
    lower_inv = factor_rows(reduced, rank, eye)[:, 2 * rank : 3 * rank]
    lower_probe = dot_high(lower_inv, probe)
    projected = dot_high(lower_inv, half)
    scale = scale_ref[...]
    prior = dot_high(projected * (scale * scale), projected, NT)

    def flat(column):
        return jnp.sum(eye * column, axis=0, keepdims=True)

    blocks = [pay_ref[i, :rank, :] for i in range(time_count)]
    side = days_dev * rank
    decay_col = []
    share = []
    for block in blocks:
        for i in range(days_dev):
            decay_col.append(block[:, side + days_dev + i : side + days_dev + i + 1])
            share.append(block[:, side + 2 * days_dev + i : side + 2 * days_dev + i + 1])
    decay_row = [flat(column) for column in decay_col]
    opening = decay_col[0] * prior * decay_row[0] + share[0] * prior
    pair = eliminate(
        [jnp.concatenate([zero, m, eye, zero], axis=1) for m in (prior, opening)], rank, False
    )
    prior_inv = pair[0][:, 2 * rank : 3 * rank]
    opening_inv = pair[1][:, 2 * rank : 3 * rank]
    cores = []
    infos = []
    for block in blocks:
        turned = dot_high(lower_inv, block)
        for i in range(days_dev):
            cores.append(turned[:, i * rank : (i + 1) * rank])
            infos.append(turned[:, side + i : side + i + 1])
    cores = dot_high(jnp.concatenate(cores, axis=0), lower_inv, NT)
    lane = lax.broadcasted_iota(jnp.int32, (rank, rank), 1)
    for t in range(days):
        rate = 1.0 / share[t]
        own = opening_inv if t == 0 else prior_inv * rate
        back = zero if t == 0 else -(prior_inv * decay_row[t]) * rate
        diagonal = own + cores[t * rank : (t + 1) * rank]
        ahead = zero
        if t + 1 < days:
            scaled = decay_col[t + 1] * prior_inv * (1.0 / share[t + 1])
            diagonal = diagonal + scaled * decay_row[t + 1]
            ahead = -scaled
        info = jnp.where(lane == 0, infos[t], 0.0)
        aug_ref[t] = jnp.concatenate([back, diagonal, ahead, info], axis=1)

    blank = jnp.zeros((reach, rank, LANES), F32)
    for ref in (low_ref, top_ref):
        ref[:reach] = blank
        ref[reach + days :] = blank
    wide = lax.broadcasted_iota(jnp.int32, (rank, LANES), 1)
    middle = (wide >= rank) & (wide < 2 * rank)
    last = wide >= 3 * rank

    def stage(index, _):
        distance = jnp.left_shift(1, index)
        mats = [aug_ref[t] for t in range(days)]
        solved = eliminate(mats, rank, False)
        for t in range(days):
            product = dot_terms_tn(aug_ref[t], solved[t])
            top = product[:rank]
            low = product[2 * rank : 3 * rank]
            top_ref[reach + t] = jnp.where(
                middle, pltpu.roll(top, rank, 1), jnp.where(wide >= 2 * rank, top, 0.0)
            )
            low_ref[reach + t] = jnp.where(
                middle,
                pltpu.roll(low, LANES - rank, 1),
                jnp.where((wide < rank) | last, low, 0.0),
            )
        for t in range(days):
            kept = jnp.where(middle | last, aug_ref[t], 0.0)
            aug_ref[t] = kept - low_ref[reach + t - distance] - top_ref[reach + t + distance]
        return _

    lax.fori_loop(0, stages, stage, 0)

    first = lax.axis_index("tm") * days_dev
    own = []
    for i in range(days_dev):
        mat = aug_ref[first + i]
        own.append(jnp.concatenate([eye, mat[:, rank:]], axis=1))
    own = [factor_rows(mat, rank, eye) for mat in eliminate(own, rank, True)]
    roots = jnp.concatenate([mat[:, :rank] for mat in own], axis=0)
    infos = [mat[:, 3 * rank : 3 * rank + 1] for mat in own]
    coefs = terms(dot_high(roots, lower_probe), 3)
    width = 8 * LANES
    for start in range(0, cells, width):
        back = back_ref[:, start : start + width]
        field = dot_16(coefs[0], back) + dot_16(coefs[1], back) + dot_16(coefs[2], back)
        for i in range(days_dev):
            part = field[i * rank : (i + 1) * rank]
            mean_ref[i : i + 1, start : start + width] = jnp.sum(
                part * infos[i], axis=0, keepdims=True
            )
            spread_ref[i : i + 1, start : start + width] = jnp.sum(
                part * part, axis=0, keepdims=True
            )


VMEM = pl.BlockSpec(memory_space=pltpu.VMEM)
PARAMS = pltpu.CompilerParams(vmem_limit_bytes=48 * 1024 * 1024)


def body(
    background, probe, member_scale, decay, inflation, obs_owner, obs_offset, obs_value, obs_weight
):
    members, rank = probe.shape
    cells = background.shape[0]
    days_dev = decay.shape[0]
    obs_dev = obs_offset.shape[1]
    space_count = lax.axis_size("space")
    time_count = lax.axis_size("tm")
    days = days_dev * time_count
    cap = 2 * obs_dev // space_count
    rows_owner = cap // LANES
    scaled = (probe.astype(F32) * member_scale[:, None]).astype(BF16)
    probe_rows = scaled.astype(F32).T
    back = background.T
    first_space = lax.axis_index("space") == 0
    extra = jnp.concatenate(
        [
            jnp.zeros((rank, days_dev), F32),
            decay.T,
            jnp.broadcast_to(inflation[None, :], (rank, days_dev)),
            jnp.zeros((rank, LANES - days_dev * rank - 3 * days_dev), F32),
        ],
        axis=1,
    )
    extra = jnp.where(first_space, extra, 0.0)

    slab = (space_count, 3 * days_dev * rows_owner, LANES)
    buckets = pl.pallas_call(
        functools.partial(bucket_kernel, space_count, cap),
        out_shape=jax.ShapeDtypeStruct(slab, F32),
        in_specs=[VMEM] * 4,
        out_specs=VMEM,
        compiler_params=PARAMS,
        name="buckets",
    )(obs_owner[:, :, 0], obs_offset, obs_value, obs_weight)
    received = pl.pallas_call(
        functools.partial(exchange_kernel, space_count),
        out_shape=jax.ShapeDtypeStruct(slab, F32),
        in_specs=[VMEM],
        out_specs=VMEM,
        scratch_shapes=[
            pltpu.SemaphoreType.DMA((space_count,)),
            pltpu.SemaphoreType.DMA((space_count,)),
            pltpu.SemaphoreType.DMA,
        ],
        compiler_params=pltpu.CompilerParams(
            collective_id=0, has_side_effects=True, vmem_limit_bytes=48 * 1024 * 1024
        ),
        name="exchange",
    )(buckets)
    payload = pl.pallas_call(
        functools.partial(info_kernel, days_dev, rows_owner),
        out_shape=jax.ShapeDtypeStruct((rank + members // 2, LANES), F32),
        in_specs=[VMEM] * 4,
        out_specs=VMEM,
        scratch_shapes=[pltpu.VMEM(((2 * days_dev + 1) * members + 16, 8 * LANES), BF16)],
        compiler_params=PARAMS,
        name="information",
    )(received, back, probe_rows, extra)
    height = payload.shape[0] // space_count
    summed = pl.pallas_call(
        functools.partial(sum_kernel, time_count, space_count),
        out_shape=jax.ShapeDtypeStruct((time_count, space_count, height, LANES), F32),
        in_specs=[VMEM],
        out_specs=VMEM,
        scratch_shapes=[
            pltpu.VMEM((space_count, height, LANES), F32),
            pltpu.VMEM((height, LANES), F32),
            pltpu.SemaphoreType.DMA((space_count,)),
            pltpu.SemaphoreType.DMA((space_count,)),
            pltpu.SemaphoreType.DMA((time_count * space_count,)),
            pltpu.SemaphoreType.DMA((time_count * space_count,)),
        ],
        compiler_params=pltpu.CompilerParams(
            collective_id=1, has_side_effects=True, vmem_limit_bytes=48 * 1024 * 1024
        ),
        name="sums",
    )(payload.reshape(space_count, height, LANES))
    reach = 1 << ((days - 1).bit_length() - 1)
    return pl.pallas_call(
        functools.partial(smooth_kernel, days_dev),
        out_shape=[jax.ShapeDtypeStruct((days_dev, cells), F32)] * 2,
        in_specs=[VMEM] * 4,
        out_specs=[VMEM] * 2,
        scratch_shapes=[
            pltpu.VMEM((days, rank, LANES), F32),
            pltpu.VMEM((days + 2 * reach, rank, LANES), F32),
            pltpu.VMEM((days + 2 * reach, rank, LANES), F32),
        ],
        compiler_params=PARAMS,
        name="smoother",
    )(summed.reshape(time_count, payload.shape[0], LANES), probe_rows, member_scale[None, :], back)


def solution(mesh):
    return jax.shard_map(
        body,
        mesh=mesh,
        in_specs=(
            P("space", None),
            P(),
            P(),
            P("tm", None),
            P("tm"),
            P("tm", "space", None),
            P("tm", "space"),
            P("tm", "space"),
            P("tm", "space"),
        ),
        out_specs=(P("tm", "space"), P("tm", "space")),
        check_vma=False,
    )
```

time: 343 us -> 66.8 us (0.19)
  blocking collectives: 106 us -> 0 us
  other arithmetic: 106 us -> 0.08 us
  local copies, waits for them, and re-layouts: 86.9 us -> 4.07 us
  Pallas kernels: 0 us -> 61.5 us
  matrix products: 29.5 us -> 0 us
  starting transfers between devices: 9.84 us -> 0 us
    another operation x47 -> x0, other arithmetic: 101 us -> none  [the longest x22 46.7 us: spd_solve(): lower_chol = jnp.linalg.cholesky(matrix)]
    all_gather x8 -> x0, blocking collectives: 68.5 us -> none  [prefix(): gathered = jax.tree.map(lambda a: lax.all_gather(a, axis), part)]
    pallas_call x0 -> x5, Pallas kernels: none -> 61.5 us  [the longest x1 29.2 us: body(): pl.pallas_call(functools.partial(smooth_kernel, days_dev), out_shape=[jax...]
    gather x2 -> x0, local copies, waits for them, and re-layouts: 47.6 us -> none  [make_reader(): basis_rows = rows_source[offsets]]
    psum x1 -> x0, blocking collectives: 37.8 us -> none  [body(): lax.psum((local_gram, core_field, vector_field), 'space')]
    dot_general x89 -> x0, matrix products: 26.3 us -> none  [the longest x85 18.6 us: matmul_high(): return jnp.matmul(left_mat, right_mat, precision=HIGHEST)]
    unnamed x26 -> x22, local copies, waits for them, and re-layouts: 25.7 us -> 3.91 us
    all_to_all x1 -> x0, starting transfers between devices: 7.25 us -> none  [body(): lax.all_to_all(buckets, 'space', split_axis=1, concat_axis=1, tiled=True)]
  transfers between devices with their start and end apart: 3 -> 0, of which waited for: 2 -> 0; matrix products, arithmetic and copies ran while one was open for 44% -> 0% of each run, Pallas kernels for 0% -> 0%
where the time goes in v1:
time: 66.8 us; the launch traced here: 66.4 us
  Pallas kernels  61.5 us (92%)
  local copies, waits for them, and re-layouts  4.07 us (6%)
  between operations  0.72 us (1%)
    pallas_call x1, Pallas kernels, body(): pl.pallas_call(functools.partial(smooth_kernel, days_dev), out_shape=[jax...  29.2 us
    pallas_call x1, Pallas kernels, body(): pl.pallas_call(functools.partial(sum_kernel, time_count, space_count), ou...  15.1 us
    pallas_call x1, Pallas kernels, body(): pl.pallas_call(functools.partial(exchange_kernel, space_count), out_shape...  9.52 us
    pallas_call x1, Pallas kernels, body(): pl.pallas_call(functools.partial(info_kernel, days_dev, rows_owner), out_...  5.8 us
    unnamed x22, local copies, waits for them, and re-layouts  3.91 us
    pallas_call x1, Pallas kernels, body(): pl.pallas_call(functools.partial(bucket_kernel, space_count, cap), out_sh...  1.9 us

profile of v1, /device:TPU:0, one launch (start us, length us, event | category | flops | bytes accessed | tf_op | source)
XLA Modules:
  0.0 66.4 jit_solution(2084429331286605817)
XLA Ops:
  0.6 0.0 copy-start.9
  0.6 0.0 copy-start.7
  0.7 0.6 copy-done.9
  1.3 0.1 pad.2.clone
  1.4 0.1 pad.3.clone
  1.4 0.0 copy-start.5
  1.4 0.0 copy-start.8
  1.5 0.0 copy-done.7
  1.5 0.6 copy-done.5
  2.1 0.0 copy-start.6
  2.1 0.0 copy-done.8
  2.1 0.0 copy-start.4
  2.1 0.1 copy.11
  2.2 0.0 copy-start.3
  2.2 0.1 maximum_select_fusion.extra_ref
  2.3 0.5 copy-done.6
  2.8 0.0 copy-start.2
  2.9 0.0 copy-done.4
  2.9 0.1 copy-done.3
  3.0 0.6 copy-done.2
  3.6 1.9 %buckets.1.in_ref = f32[8,36,128]{2,1,0:T(8,128)S(1)} custom-call(s32[3,2048]{1,0:T(4,128)S(1)} %bitcast.14, s32[3,2048]{1,0:T(4,128)S(1)} %copy-done.2, f32[3,2048]{1,0:T(4,128)S(1)} %copy-done.3, f32[3,2048]{1,0:T(4,128)S(1)} %copy-done.4), custom_call_target="tpu_custom_call" | custom-call | tf_op jit(solution)/shard_map/buckets/pallas_call | solution.py:449
  5.5 9.5 %exchange.1.got_ref = f32[8,36,128]{2,1,0:T(8,128)S(1)} custom-call(f32[8,36,128]{2,1,0:T(8,128)S(1)} %buckets.1.in_ref), custom_call_target="tpu_custom_call" | custom-call | tf_op jit(solution)/shard_map/exchange/pallas_call | solution.py:457
  15.0 0.0 copy-start
  15.1 1.2 %copy-done = bf16[8192,64]{0,1:T(8,128)(2,1)S(1)} copy-done((bf16[8192,64]{0,1:T(8,128)(2,1)S(1)}, bf16[8192,64]{0,1:T(8,128)(2,1)}, u32[]{:S(2)}) %copy-start) | copy-done | bytes 1048600
  16.3 0.0 copy-start.1
  16.3 5.8 %information.1 = f32[64,128]{1,0:T(8,128)S(1)} custom-call(f32[8,36,128]{2,1,0:T(8,128)S(1)} %exchange.1.got_ref, bf16[64,8192]{1,0:T(8,128)(2,1)S(1)} %bitcast.10, f32[32,64]{1,0:T(8,128)S(1)} %convert_bitcast_fusion.probe_ref, f32[32,32]{1,0:T(8,128)S(1)} %maximum_select_fusion.extra_ref), custom_call_target="tpu_custom_call" | custom-call | tf_op jit(solution)/shard_map/information/pallas_call | solution.py:472
  22.1 15.1 %sums.1 = f32[4,8,8,128]{3,2,1,0:T(8,128)S(1)} custom-call(f32[8,8,128]{2,1,0:T(8,128)S(1)} %bitcast.13), custom_call_target="tpu_custom_call" | custom-call | tf_op jit(solution)/shard_map/sums/pallas_call | solution.py:482
  37.2 0.0 copy-done.1
  37.2 29.2 %smoother.1 = (f32[3,8192]{1,0:T(4,128)}, f32[3,8192]{1,0:T(4,128)}) custom-call(f32[4,64,128]{2,1,0:T(8,128)S(1)} %bitcast.12, f32[32,64]{1,0:T(8,128)S(1)} %convert_bitcast_fusion.probe_ref, f32[1,64]{1,0:T(1,128)S(1)} %bitcast.15, bf16[64,8192]{1,0:T(8,128)(2,1)S(1)} %bitcast.11), custom_call_target="tpu_custom_call" | custom-call | tf_op jit(solution)/shard_map/smoother/pallas_call | solution.py:501
  (5 shorter events, 0.0 us)
Async XLA Ops:
  0.6 0.7 copy-start.9
  0.6 0.8 %copy-start.7 = (bf16[64,32]{0,1:T(8,128)(2,1)S(1)}, bf16[64,32]{0,1:T(8,128)(2,1)}, u32[]{:S(2)}) copy-start(bf16[64,32]{0,1:T(8,128)(2,1)} %param.10) | copy-start | bytes 12292
  1.4 0.7 copy-start.5
  1.4 0.7 %copy-start.8 = (f32[3,32]{1,0:T(4,128)S(1)}, f32[3,32]{1,0:T(4,128)}, u32[]{:S(2)}) copy-start(f32[3,32]{1,0:T(4,128)} %param.12) | copy-start | bytes 1156
  2.1 0.7 %copy-start.6 = (s32[3,2048,1]{1,2,0:T(1,128)S(1)}, s32[3,2048,1]{1,2,0:T(1,128)}, u32[]{:S(2)}) copy-start(s32[3,2048,1]{1,2,0:T(1,128)} %param.14) | copy-start | bytes 73732
  2.1 0.8 %copy-start.4 = (f32[3,2048]{1,0:T(4,128)S(1)}, f32[3,2048]{1,0:T(4,128)}, u32[]{:S(2)}) copy-start(f32[3,2048]{1,0:T(4,128)} %weight_ref.1) | copy-start | bytes 73732
  2.2 0.8 %copy-start.3 = (f32[3,2048]{1,0:T(4,128)S(1)}, f32[3,2048]{1,0:T(4,128)}, u32[]{:S(2)}) copy-start(f32[3,2048]{1,0:T(4,128)} %value_ref.1) | copy-start | bytes 73732
  2.8 0.8 %copy-start.2 = (s32[3,2048]{1,0:T(4,128)S(1)}, s32[3,2048]{1,0:T(4,128)}, u32[]{:S(2)}) copy-start(s32[3,2048]{1,0:T(4,128)} %offset_ref.1) | copy-start | bytes 73732
  15.0 1.2 %copy-start = (bf16[8192,64]{0,1:T(8,128)(2,1)S(1)}, bf16[8192,64]{0,1:T(8,128)(2,1)}, u32[]{:S(2)}) copy-start(bf16[8192,64]{0,1:T(8,128)(2,1)} %param.9) | copy-start | bytes 3145732
  16.3 20.9 %copy-start.1 = (bf16[8192,64]{0,1:T(8,128)(2,1)S(1)}, bf16[8192,64]{0,1:T(8,128)(2,1)}, u32[]{:S(2)}) copy-start(bf16[8192,64]{0,1:T(8,128)(2,1)} %param.9) | copy-start | bytes 3145732

commit v2 on v1

--- a/solution.py
+++ b/solution.py
@@ -46,8 +46,8 @@
     )
 
 
-def bucket_kernel(space_count, cap, owner_ref, offset_ref, value_ref, weight_ref, out_ref):
-    days, count = owner_ref.shape
+def make_buckets(space_count, cap, owner_ref, offset_ref, value_ref, weight_ref, out_ref):
+    days, count = offset_ref.shape
     chunks = count // LANES
     rows_owner = cap // LANES
     slot_rows = space_count * rows_owner
@@ -59,17 +59,16 @@
     for day in range(days):
         hits = []
         for chunk in range(chunks):
-            own = owner_ref[day : day + 1, chunk * LANES : (chunk + 1) * LANES]
+            own = owner_ref[day, :, chunk * LANES : (chunk + 1) * LANES]
             hits.append((owner_row == own).astype(F32))
         stacked = jnp.concatenate(hits, axis=0).astype(BF16)
         inside = dot_16(stacked, earlier)
         totals = dot_16(stacked, ones)
-        base = jnp.zeros((space_count, LANES), F32)
+        base = (owner_row * cap).astype(F32)
         slots = []
-        owner_start = (owner_row * cap).astype(F32)
         for chunk in range(chunks):
             part = slice(chunk * space_count, (chunk + 1) * space_count)
-            place = hits[chunk] * (inside[part] + base + owner_start)
+            place = hits[chunk] * (inside[part] + base)
             slots.append(jnp.sum(place, axis=0, keepdims=True))
             base = base + totals[part]
         slot = jnp.concatenate(slots, axis=1).astype(jnp.int32)
@@ -100,123 +99,110 @@
                 ]
 
 
-def greet(peers_of, count):
-    barrier = pltpu.get_barrier_semaphore()
-
-    def signal(step, _):
-        pl.semaphore_signal(barrier, inc=1, device_id=peers_of(step), device_id_type=MESH)
-        return _
-
-    lax.fori_loop(1, count, signal, 0)
-    pl.semaphore_wait(barrier, count - 1)
-
-
-def exchange_kernel(space_count, in_ref, out_ref, send_sem, recv_sem, own_sem):
-    time_index = lax.axis_index("tm")
-    me = lax.axis_index("space")
-
-    def peer(step):
-        return lax.rem(me + step, space_count)
-
-    greet(lambda step: (time_index, peer(step)), space_count)
-
-    def copy(step):
-        return pltpu.make_async_remote_copy(
-            src_ref=in_ref.at[peer(step)],
-            dst_ref=out_ref.at[me],
-            send_sem=send_sem.at[step],
-            recv_sem=recv_sem.at[step],
-            device_id=(time_index, peer(step)),
-            device_id_type=MESH,
-        )
-
-    own = pltpu.make_async_copy(in_ref.at[me], out_ref.at[me], own_sem)
-    for step in range(1, space_count):
-        copy(step).start()
-    own.start()
-    own.wait()
-    for step in range(1, space_count):
-        copy(step).wait()
-
-
-def sum_kernel(
-    time_count, space_count, in_ref, out_ref, held, total, send_sem, recv_sem, send_all, recv_all
+def gather_kernel(
+    time_count,
+    space_count,
+    cap,
+    owner_hbm,
+    offset_hbm,
+    value_hbm,
+    weight_hbm,
+    back_hbm,
+    probe_ref,
+    extra_ref,
+    out_ref,
+    owner_ref,
+    offset_ref,
+    value_ref,
+    weight_ref,
+    back_ref,
+    sent,
+    got,
+    weighted,
+    hists,
+    payload,
+    held,
+    local_sem,
+    send_sem,
+    recv_sem,
+    send_sum,
+    recv_sum,
+    send_time,
+    recv_time,
+    send_all,
+    recv_all,
 ):
     time_index = lax.axis_index("tm")
     me = lax.axis_index("space")
-    device_count = time_count * space_count
-
-    def peer(step):
-        return lax.rem(me + step, space_count)
-
-    def any_peer(step):
-        time_peer = lax.rem(time_index + step // space_count, time_count)
-        return (time_peer, lax.rem(me + lax.rem(step, space_count), space_count))
-
-    greet(any_peer, device_count)
-
-    def copy(step):
-        return pltpu.make_async_remote_copy(
-            src_ref=in_ref.at[peer(step)],
-            dst_ref=held.at[step],
-            send_sem=send_sem.at[step],
-            recv_sem=recv_sem.at[step],
-            device_id=(time_index, peer(step)),
-            device_id_type=MESH,
-        )
-
-    for step in range(1, space_count):
-        copy(step).start()
-    added = in_ref[me]
-    for step in range(1, space_count):
-        copy(step).wait()
-        added = added + held[step]
-    total[...] = added
-    out_ref[time_index, me] = added
-
-    def share(step):
-        return pltpu.make_async_remote_copy(
-            src_ref=total,
-            dst_ref=out_ref.at[time_index, me],
-            send_sem=send_all.at[step],
-            recv_sem=recv_all.at[step],
-            device_id=any_peer(step),
-            device_id_type=MESH,
-        )
-
-    def start(step, _):
-        share(step).start()
-        return _
-
-    def wait(step, _):
-        share(step).wait()
-        return _
-
-    lax.fori_loop(1, device_count, start, 0)
-    lax.fori_loop(1, device_count, wait, 0)
-
-
-def info_kernel(days, rows_owner, got_ref, back_ref, probe_ref, extra_ref, out_ref, weighted):
-    readers = got_ref.shape[0]
+    days = offset_ref.shape[0]
+    rows_owner = cap // LANES
     members, cells = back_ref.shape
     rank = probe_ref.shape[0]
     high_count = cells // LANES
-    step_rows = 8
-    slots = step_rows * LANES
+
+    def space_peer(step):
+        return (time_index, lax.rem(me + step, space_count))
+
+    def time_peer(step):
+        return (lax.rem(time_index + step, time_count), me)
+
+    loads = [
+        pltpu.make_async_copy(source, target, local_sem.at[i])
+        for i, (source, target) in enumerate(
+            (
+                (owner_hbm, owner_ref),
+                (offset_hbm, offset_ref),
+                (value_hbm, value_ref),
+                (weight_hbm, weight_ref),
+                (back_hbm, back_ref),
+            )
+        )
+    ]
+    for load in loads:
+        load.start()
+    barrier = pltpu.get_barrier_semaphore()
+    for step in range(1, space_count):
+        pl.semaphore_signal(barrier, inc=1, device_id=space_peer(step), device_id_type=MESH)
+    for step in range(1, time_count):
+        pl.semaphore_signal(barrier, inc=1, device_id=time_peer(step), device_id_type=MESH)
+    for load in loads[:4]:
+        load.wait()
+    make_buckets(space_count, cap, owner_ref, offset_ref, value_ref, weight_ref, sent)
+    pl.semaphore_wait(barrier, space_count + time_count - 2)
+
+    def space_copy(step, source, target, sends, receives):
+        return pltpu.make_async_remote_copy(
+            src_ref=source,
+            dst_ref=target,
+            send_sem=sends.at[step],
+            recv_sem=receives.at[step],
+            device_id=space_peer(step),
+            device_id_type=MESH,
+        )
+
+    copies = [
+        space_copy(step, sent.at[space_peer(step)[1]], got.at[step], send_sem, recv_sem)
+        for step in range(1, space_count)
+    ]
+    for copy in copies:
+        copy.start()
+    loads[4].wait()
+
+    slots = rows_owner * LANES
     high_row = lax.broadcasted_iota(jnp.int32, (high_count, slots), 0)
     low_row = lax.broadcasted_iota(jnp.int32, (LANES, slots), 0)
-    weight_maps = []
-    value_maps = []
-    for day in range(days):
-        hist = jnp.zeros((4 * high_count, LANES), F32)
-        places = [(r, j) for r in range(readers) for j in range(rows_owner)]
-        for first in range(0, len(places), step_rows):
-            group = places[first : first + step_rows]
+    for step in range(space_count):
+        if step > 0:
+            copies[step - 1].wait()
+            slab = got[step]
+        else:
+            slab = sent[me]
+        for day in range(days):
 
             def rows(kind):
                 start = (kind * days + day) * rows_owner
                 return jnp.concatenate(
-                    [got_ref[r, start + j : start + j + 1, :] for r, j in group], axis=1
+                    [slab[start + j : start + j + 1, :] for j in range(rows_owner)], axis=1
                 )
 
             weight = rows(0)
@@ -231,7 +217,12 @@
                 axis=0,
             )
             right = (low_row == low).astype(F32).astype(BF16)
-            hist = hist + dot_16(left, right, NT)
+            part = dot_16(left, right, NT)
+            hists[day] = part if step == 0 else hists[day] + part
+    weight_maps = []
+    value_maps = []
+    for day in range(days):
+        hist = hists[day]
         weight_maps.append(hist[:high_count] + hist[high_count : 2 * high_count])
         value_maps.append(hist[2 * high_count : 3 * high_count] + hist[3 * high_count :])
 
@@ -262,32 +253,87 @@
         sums = sums + dot_16(weighted[...], back, NT)
 
     probe = probe_ref[...]
-    columns = []
-    for day in range(days):
-        info = sums[2 * day * members : (2 * day + 1) * members]
-        info = info + sums[(2 * day + 1) * members : (2 * day + 2) * members]
-        columns.append(dot_high(dot_high(probe, info), probe, NT))
+    infos = [
+        sums[2 * day * members : (2 * day + 1) * members]
+        + sums[(2 * day + 1) * members : (2 * day + 2) * members]
+        for day in range(days)
+    ]
+    turned = dot_high(jnp.concatenate(infos, axis=0), probe, NT)
+    columns = [
+        dot_high(probe, turned[day * members : (day + 1) * members]) for day in range(days)
+    ]
     gram = sums[2 * days * members : (2 * days + 1) * members]
     tail = sums[(2 * days + 1) * members :]
     vector_rows = tail[:8] + tail[8:]
     side = LANES - days * rank
     vector_rows = jnp.concatenate([vector_rows, jnp.zeros((side - 8, members), F32)], axis=0)
     columns.append(dot_high(probe, vector_rows, NT) + extra_ref[...])
-    out_ref[:rank, :] = jnp.concatenate(columns, axis=1)
-    out_ref[rank:, :] = jnp.concatenate([gram[:rank], gram[rank:]], axis=1)
+    upper = jnp.concatenate(columns, axis=1)
+    lower = jnp.concatenate([gram[:rank], gram[rank:]], axis=1)
+    height = payload.shape[1]
+    for i in range(space_count):
+        start = i * height
+        payload[i] = (
+            upper[start : start + height] if start < rank else lower[start - rank : start - rank + height]
+        )
+
+    copies = [
+        space_copy(step, payload.at[space_peer(step)[1]], held.at[step], send_sum, recv_sum)
+        for step in range(1, space_count)
+    ]
+    for copy in copies:
+        copy.start()
+    added = payload[me]
+    for step in range(1, space_count):
+        copies[step - 1].wait()
+        added = added + held[step]
+    out_ref[me, time_index] = added
+    copies = [
+        pltpu.make_async_remote_copy(
+            src_ref=out_ref.at[me, time_index],
+            dst_ref=out_ref.at[me, time_index],
+            send_sem=send_time.at[step],
+            recv_sem=recv_time.at[step],
+            device_id=time_peer(step),
+            device_id_type=MESH,
+        )
+        for step in range(1, time_count)
+    ]
+    for copy in copies:
+        copy.start()
+    for copy in copies:
+        copy.wait()
+    copies = [
+        space_copy(step, out_ref.at[me], out_ref.at[me], send_all, recv_all)
+        for step in range(1, space_count)
+    ]
+    for copy in copies:
+        copy.start()
+    for copy in copies:
+        copy.wait()
 
 
 def eliminate(mats, rank, only_below):
     row = lax.broadcasted_iota(jnp.int32, (rank, LANES), 0)
     mats = list(mats)
-    for k in range(rank):
+    for k in range(0, rank, 2):
         for i, mat in enumerate(mats):
-            col = mat[:, rank + k : rank + k + 1]
-            scaled = mat[k : k + 1, :] * (1.0 / col[k : k + 1, :])
+            col_a = mat[:, rank + k : rank + k + 1]
+            col_b = mat[:, rank + k + 1 : rank + k + 2]
+            a, b = col_a[k : k + 1, :], col_b[k : k + 1, :]
+            c = col_b[k + 1 : k + 2, :]
+            row_a, row_b = mat[k : k + 1, :], mat[k + 1 : k + 2, :]
+            scale = 1.0 / (a * c - b * b)
+            new_a = (c * row_a - b * row_b) * scale
+            new_b = (a * row_b - b * row_a) * scale
+            update = mat - col_a * new_a - col_b * new_b
             if only_below:
-                mats[i] = mat - jnp.where(row > k, col, 0.0) * scaled
+                second = row_b - (b / a) * row_a
+                mats[i] = jnp.where(
+                    row > k + 1, update, jnp.where(row == k + 1, second, mat)
+                )
             else:
-                mats[i] = jnp.where(row == k, scaled, mat - col * scaled)
+                mats[i] = jnp.where(row == k, new_a, jnp.where(row == k + 1, new_b, update))
     return mats
 
 
@@ -297,9 +343,22 @@
 
 
 def smooth_kernel(
-    days_dev, pay_ref, probe_ref, scale_ref, back_ref, mean_ref, spread_ref, aug_ref, low_ref, top_ref
+    days_dev,
+    pay_ref,
+    probe_ref,
+    scale_ref,
+    back_hbm,
+    mean_ref,
+    spread_ref,
+    aug_ref,
+    low_ref,
+    top_ref,
+    back_ref,
+    back_sem,
 ):
-    time_count = pay_ref.shape[0]
+    load = pltpu.make_async_copy(back_hbm, back_ref, back_sem)
+    load.start()
+    space_count, time_count, height = pay_ref.shape[:3]
     rank, members = probe_ref.shape
     cells = back_ref.shape[1]
     days = time_count * days_dev
@@ -309,7 +368,10 @@
     eye = (rows == lax.broadcasted_iota(jnp.int32, (rank, rank), 1)).astype(F32)
     zero = jnp.zeros((rank, rank), F32)
     probe = probe_ref[...]
-    gram_pair = pay_ref[0, rank:, :]
+    upper_count = rank // height
+    gram_pair = jnp.concatenate(
+        [pay_ref[s, 0] for s in range(upper_count, space_count)], axis=0
+    )
     gram = jnp.concatenate([gram_pair[:, :members], gram_pair[:, members:]], axis=0)
     half = dot_high(probe, gram)
     core_gram = dot_high(half, probe, NT)
@@ -323,7 +385,10 @@
     def flat(column):
         return jnp.sum(eye * column, axis=0, keepdims=True)
 
-    blocks = [pay_ref[i, :rank, :] for i in range(time_count)]
+    blocks = [
+        jnp.concatenate([pay_ref[s, i] for s in range(upper_count)], axis=0)
+        for i in range(time_count)
+    ]
     side = days_dev * rank
     decay_col = []
     share = []
@@ -401,6 +466,7 @@
     infos = [mat[:, 3 * rank : 3 * rank + 1] for mat in own]
     coefs = terms(dot_high(roots, lower_probe), 3)
     width = 8 * LANES
+    load.wait()
     for start in range(0, cells, width):
         back = back_ref[:, start : start + width]
         field = dot_16(coefs[0], back) + dot_16(coefs[1], back) + dot_16(coefs[2], back)
@@ -415,7 +481,8 @@
 
 
 VMEM = pl.BlockSpec(memory_space=pltpu.VMEM)
-PARAMS = pltpu.CompilerParams(vmem_limit_bytes=48 * 1024 * 1024)
+ANY = pl.BlockSpec(memory_space=pl.ANY)
+PARAMS = pltpu.CompilerParams(vmem_limit_bytes=56 * 1024 * 1024)
 
 
 def body(
@@ -446,71 +513,65 @@
     extra = jnp.where(first_space, extra, 0.0)
 
     slab = (space_count, 3 * days_dev * rows_owner, LANES)
-    buckets = pl.pallas_call(
-        functools.partial(bucket_kernel, space_count, cap),
-        out_shape=jax.ShapeDtypeStruct(slab, F32),
-        in_specs=[VMEM] * 4,
-        out_specs=VMEM,
-        compiler_params=PARAMS,
-        name="buckets",
-    )(obs_owner[:, :, 0], obs_offset, obs_value, obs_weight)
-    received = pl.pallas_call(
-        functools.partial(exchange_kernel, space_count),
-        out_shape=jax.ShapeDtypeStruct(slab, F32),
-        in_specs=[VMEM],
+    height = (rank + members // 2) // space_count
+    part = (space_count, height, LANES)
+    dma = pltpu.SemaphoreType.DMA
+    summed = pl.pallas_call(
+        functools.partial(gather_kernel, time_count, space_count, cap),
+        out_shape=jax.ShapeDtypeStruct((space_count, time_count, height, LANES), F32),
+        in_specs=[ANY] * 5 + [VMEM] * 2,
         out_specs=VMEM,
         scratch_shapes=[
-            pltpu.SemaphoreType.DMA((space_count,)),
-            pltpu.SemaphoreType.DMA((space_count,)),
-            pltpu.SemaphoreType.DMA,
+            pltpu.VMEM((days_dev, 1, obs_dev), jnp.int32),
+            pltpu.VMEM((days_dev, obs_dev), jnp.int32),
+            pltpu.VMEM((days_dev, obs_dev), F32),
+            pltpu.VMEM((days_dev, obs_dev), F32),
+            pltpu.VMEM((members, cells), BF16),
+            pltpu.VMEM(slab, F32),
+            pltpu.VMEM(slab, F32),
+            pltpu.VMEM(((2 * days_dev + 1) * members + 16, 8 * LANES), BF16),
+            pltpu.VMEM((days_dev, 4 * (cells // LANES), LANES), F32),
+            pltpu.VMEM(part, F32),
+            pltpu.VMEM(part, F32),
+            dma((5,)),
+            dma((space_count,)),
+            dma((space_count,)),
+            dma((space_count,)),
+            dma((space_count,)),
+            dma((time_count,)),
+            dma((time_count,)),
+            dma((space_count,)),
+            dma((space_count,)),
         ],
         compiler_params=pltpu.CompilerParams(
-            collective_id=0, has_side_effects=True, vmem_limit_bytes=48 * 1024 * 1024
+            collective_id=0, has_side_effects=True, vmem_limit_bytes=56 * 1024 * 1024
         ),
-        name="exchange",
-    )(buckets)
-    payload = pl.pallas_call(
-        functools.partial(info_kernel, days_dev, rows_owner),
-        out_shape=jax.ShapeDtypeStruct((rank + members // 2, LANES), F32),
-        in_specs=[VMEM] * 4,
-        out_specs=VMEM,
-        scratch_shapes=[pltpu.VMEM(((2 * days_dev + 1) * members + 16, 8 * LANES), BF16)],
-        compiler_params=PARAMS,
-        name="information",
-    )(received, back, probe_rows, extra)
-    height = payload.shape[0] // space_count
-    summed = pl.pallas_call(
-        functools.partial(sum_kernel, time_count, space_count),
-        out_shape=jax.ShapeDtypeStruct((time_count, space_count, height, LANES), F32),
-        in_specs=[VMEM],
-        out_specs=VMEM,
-        scratch_shapes=[
-            pltpu.VMEM((space_count, height, LANES), F32),
-            pltpu.VMEM((height, LANES), F32),
-            pltpu.SemaphoreType.DMA((space_count,)),
-            pltpu.SemaphoreType.DMA((space_count,)),
-            pltpu.SemaphoreType.DMA((time_count * space_count,)),
-            pltpu.SemaphoreType.DMA((time_count * space_count,)),
-        ],
-        compiler_params=pltpu.CompilerParams(
-            collective_id=1, has_side_effects=True, vmem_limit_bytes=48 * 1024 * 1024
-        ),
-        name="sums",
-    )(payload.reshape(space_count, height, LANES))
+        name="gather",
+    )(
+        jnp.swapaxes(obs_owner, 1, 2),
+        obs_offset,
+        obs_value,
+        obs_weight,
+        back,
+        probe_rows,
+        extra,
+    )
     reach = 1 << ((days - 1).bit_length() - 1)
     return pl.pallas_call(
         functools.partial(smooth_kernel, days_dev),
         out_shape=[jax.ShapeDtypeStruct((days_dev, cells), F32)] * 2,
-        in_specs=[VMEM] * 4,
+        in_specs=[VMEM] * 3 + [ANY],
         out_specs=[VMEM] * 2,
         scratch_shapes=[
             pltpu.VMEM((days, rank, LANES), F32),
             pltpu.VMEM((days + 2 * reach, rank, LANES), F32),
             pltpu.VMEM((days + 2 * reach, rank, LANES), F32),
+            pltpu.VMEM((members, cells), BF16),
+            pltpu.SemaphoreType.DMA,
         ],
         compiler_params=PARAMS,
         name="smoother",
-    )(summed.reshape(time_count, payload.shape[0], LANES), probe_rows, member_scale[None, :], back)
+    )(summed, probe_rows, member_scale[None, :], back)
 
 
 def solution(mesh):

time: 66.8 us -> 110 us (1.65)
  Pallas kernels: 61.5 us -> 106 us
  local copies, waits for them, and re-layouts: 4.07 us -> 1.62 us
  other arithmetic: 0.08 us -> 1.29 us
    pallas_call x1, Pallas kernels: 29.2 us -> 74.4 us  [body(): pl.pallas_call(functools.partial(smooth_kernel, days_dev), out_shape=[jax...]
    unnamed x22 -> x9, local copies, waits for them, and re-layouts: 3.91 us -> 1.46 us
    pallas_call x4 -> x1, Pallas kernels: 32.4 us -> 31.4 us  [body(): pl.pallas_call(functools.partial(gather_kernel, time_count, space_count,...]
where the time goes in v2:
time: 110 us; the launch traced here: 109 us
  Pallas kernels  106 us (96%)
  local copies, waits for them, and re-layouts  1.62 us (1%)
  other arithmetic  1.29 us (1%)
    pallas_call x1, Pallas kernels, body(): pl.pallas_call(functools.partial(smooth_kernel, days_dev), out_shape=[jax...  74.4 us
    pallas_call x1, Pallas kernels, body(): pl.pallas_call(functools.partial(gather_kernel, time_count, space_count,...  31.4 us

profile of v2, /device:TPU:0, one launch (start us, length us, event | category | flops | bytes accessed | tf_op | source)
XLA Modules:
  0.0 109.5 jit_solution(15447125739259396227)
XLA Ops:
  0.6 0.0 copy-start.3
  0.6 0.0 copy-start
  0.7 0.6 copy-done.3
  1.3 0.1 pad.2.clone
  1.4 0.1 pad.3.clone
  1.4 0.0 copy-start.1
  1.5 0.0 copy-done
  1.5 0.6 copy-done.1
  2.1 0.0 copy-start.2
  2.1 0.6 convert_bitcast_fusion.probe_ref
  2.7 0.1 copy-done.2
  2.8 0.1 copy.11
  2.9 0.7 maximum_select_fusion.extra_ref
  3.6 31.4 %gather.1.pay_ref = f32[8,4,8,128]{3,2,1,0:T(8,128)} custom-call(s32[3,1,2048]{2,1,0:T(1,128)} %bitcast.9, s32[3,2048]{1,0:T(4,128)} %offset_hbm.1, f32[3,2048]{1,0:T(4,128)} %value_hbm.1, f32[3,2048]{1,0:T(4,128)} %weight_hbm.1, bf16[64,8192]{1,0:T(8,128)(2,1)} %bitcast.6, f32[32,64]{1,0:T(8,128)} %convert_bitcast_fusion.probe_ref, ...), custom_call_target="tpu_custom_call" | custom-call | tf_op jit(solution)/shard_map/gather/pallas_call | solution.py:519
  35.0 74.4 %smoother.1 = (f32[3,8192]{1,0:T(4,128)}, f32[3,8192]{1,0:T(4,128)}) custom-call(f32[8,4,8,128]{3,2,1,0:T(8,128)} %gather.1.pay_ref, f32[32,64]{1,0:T(8,128)} %convert_bitcast_fusion.probe_ref, f32[1,64]{1,0:T(1,128)} %bitcast.10, bf16[64,8192]{1,0:T(8,128)(2,1)} %bitcast.7), custom_call_target="tpu_custom_call" | custom-call | tf_op jit(solution)/shard_map/smoother/pallas_call | solution.py:560
  (3 shorter events, 0.0 us)
Async XLA Ops:
  0.6 0.7 copy-start.3
  0.6 0.8 copy-start
  1.4 0.7 copy-start.1
  2.1 0.7 copy-start.2

commit v3 on v2

--- a/solution.py
+++ b/solution.py
@@ -44,6 +44,11 @@
         jnp.concatenate([r1, r2, r1, r2, r3, r1], axis=0),
         TN,
     )
+
+
+def scaled_rows(probe_ref, scale_ref):
+    scaled = (probe_ref[...].astype(F32) * scale_ref[...]).astype(BF16)
+    return scaled.astype(F32)
 
 
 def make_buckets(space_count, cap, owner_ref, offset_ref, value_ref, weight_ref, out_ref):
@@ -108,14 +113,20 @@
     value_hbm,
     weight_hbm,
     back_hbm,
-    probe_ref,
-    extra_ref,
+    probe_hbm,
+    scale_hbm,
+    decay_hbm,
+    inflation_hbm,
     out_ref,
     owner_ref,
     offset_ref,
     value_ref,
     weight_ref,
     back_ref,
+    probe_ref,
+    scale_ref,
+    decay_ref,
+    inflation_ref,
     sent,
     got,
     weighted,
@@ -155,6 +166,10 @@
                 (value_hbm, value_ref),
                 (weight_hbm, weight_ref),
                 (back_hbm, back_ref),
+                (probe_hbm, probe_ref),
+                (scale_hbm, scale_ref),
+                (decay_hbm, decay_ref),
+                (inflation_hbm, inflation_ref),
             )
         )
     ]
@@ -186,7 +201,21 @@
     ]
     for copy in copies:
         copy.start()
-    loads[4].wait()
+    for load in loads[4:]:
+        load.wait()
+    probe = scaled_rows(probe_ref, scale_ref)
+    at_row = lax.broadcasted_iota(jnp.int32, (rank, rank), 0)
+    at_lane = lax.broadcasted_iota(jnp.int32, (rank, rank), 1)
+    side = LANES - days * rank
+    side_lane = lax.broadcasted_iota(jnp.int32, (rank, side), 1)
+    extra = jnp.zeros((rank, side), F32)
+    for day in range(days):
+        line = jnp.where(at_row == at_lane, decay_ref[day : day + 1, :], 0.0)
+        column = jnp.sum(line, axis=1, keepdims=True)
+        extra = jnp.where(side_lane == days + day, column, extra)
+        share = inflation_ref[:, day : day + 1]
+        extra = jnp.where(side_lane == 2 * days + day, share, extra)
+    extra = extra * (me == 0).astype(F32)
 
     slots = rows_owner * LANES
     high_row = lax.broadcasted_iota(jnp.int32, (high_count, slots), 0)
@@ -252,7 +281,6 @@
         weighted[(2 * days + 1) * members :, :] = vectors.astype(BF16)
         sums = sums + dot_16(weighted[...], back, NT)
 
-    probe = probe_ref[...]
     infos = [
         sums[2 * day * members : (2 * day + 1) * members]
         + sums[(2 * day + 1) * members : (2 * day + 2) * members]
@@ -265,9 +293,8 @@
     gram = sums[2 * days * members : (2 * days + 1) * members]
     tail = sums[(2 * days + 1) * members :]
     vector_rows = tail[:8] + tail[8:]
-    side = LANES - days * rank
     vector_rows = jnp.concatenate([vector_rows, jnp.zeros((side - 8, members), F32)], axis=0)
-    columns.append(dot_high(probe, vector_rows, NT) + extra_ref[...])
+    columns.append(dot_high(probe, vector_rows, NT) + extra)
     upper = jnp.concatenate(columns, axis=1)
     lower = jnp.concatenate([gram[:rank], gram[rank:]], axis=1)
     height = payload.shape[1]
@@ -314,27 +341,44 @@
 
 
 def eliminate(mats, rank, only_below):
-    row = lax.broadcasted_iota(jnp.int32, (rank, LANES), 0)
-    mats = list(mats)
+    tile = (8, LANES)
+    row = lax.broadcasted_iota(jnp.int32, tile, 0)
+    count = rank // 8
+    all_tiles = [[mat[8 * j : 8 * j + 8, :] for j in range(count)] for mat in mats]
+
+    def spread_row(value, index):
+        return jnp.broadcast_to(value[index : index + 1, :], tile)
+
+    def spread_lane(value, index):
+        return jnp.broadcast_to(value[:, index : index + 1], tile)
+
     for k in range(0, rank, 2):
-        for i, mat in enumerate(mats):
-            col_a = mat[:, rank + k : rank + k + 1]
-            col_b = mat[:, rank + k + 1 : rank + k + 2]
-            a, b = col_a[k : k + 1, :], col_b[k : k + 1, :]
-            c = col_b[k + 1 : k + 2, :]
-            row_a, row_b = mat[k : k + 1, :], mat[k + 1 : k + 2, :]
+        own, at = k // 8, k % 8
+        for tiles in all_tiles:
+            active = range(own, count) if only_below else range(count)
+            col_a = {j: spread_lane(tiles[j], rank + k) for j in active}
+            col_b = {j: spread_lane(tiles[j], rank + k + 1) for j in active}
+            row_a, row_b = spread_row(tiles[own], at), spread_row(tiles[own], at + 1)
+            a, b = spread_row(col_a[own], at), spread_row(col_b[own], at)
+            c = spread_row(col_b[own], at + 1)
             scale = 1.0 / (a * c - b * b)
             new_a = (c * row_a - b * row_b) * scale
             new_b = (a * row_b - b * row_a) * scale
-            update = mat - col_a * new_a - col_b * new_b
             if only_below:
                 second = row_b - (b / a) * row_a
-                mats[i] = jnp.where(
-                    row > k + 1, update, jnp.where(row == k + 1, second, mat)
-                )
-            else:
-                mats[i] = jnp.where(row == k, new_a, jnp.where(row == k + 1, new_b, update))
-    return mats
+            for j in active:
+                update = tiles[j] - col_a[j] * new_a - col_b[j] * new_b
+                if j != own:
+                    tiles[j] = update
+                elif only_below:
+                    tiles[j] = jnp.where(
+                        row > at + 1, update, jnp.where(row == at + 1, second, tiles[j])
+                    )
+                else:
+                    tiles[j] = jnp.where(
+                        row == at, new_a, jnp.where(row == at + 1, new_b, update)
+                    )
+    return [jnp.concatenate(tiles, axis=0) for tiles in all_tiles]
 
 
 def factor_rows(mat, rank, eye):
@@ -367,7 +411,7 @@
     rows = lax.broadcasted_iota(jnp.int32, (rank, rank), 0)
     eye = (rows == lax.broadcasted_iota(jnp.int32, (rank, rank), 1)).astype(F32)
     zero = jnp.zeros((rank, rank), F32)
-    probe = probe_ref[...]
+    probe = scaled_rows(probe_ref, scale_ref)
     upper_count = rank // height
     gram_pair = jnp.concatenate(
         [pay_ref[s, 0] for s in range(upper_count, space_count)], axis=0
@@ -497,21 +541,9 @@
     days = days_dev * time_count
     cap = 2 * obs_dev // space_count
     rows_owner = cap // LANES
-    scaled = (probe.astype(F32) * member_scale[:, None]).astype(BF16)
-    probe_rows = scaled.astype(F32).T
+    probe_rows = probe.T
+    scale_row = member_scale[None, :]
     back = background.T
-    first_space = lax.axis_index("space") == 0
-    extra = jnp.concatenate(
-        [
-            jnp.zeros((rank, days_dev), F32),
-            decay.T,
-            jnp.broadcast_to(inflation[None, :], (rank, days_dev)),
-            jnp.zeros((rank, LANES - days_dev * rank - 3 * days_dev), F32),
-        ],
-        axis=1,
-    )
-    extra = jnp.where(first_space, extra, 0.0)
-
     slab = (space_count, 3 * days_dev * rows_owner, LANES)
     height = (rank + members // 2) // space_count
     part = (space_count, height, LANES)
@@ -519,7 +551,7 @@
     summed = pl.pallas_call(
         functools.partial(gather_kernel, time_count, space_count, cap),
         out_shape=jax.ShapeDtypeStruct((space_count, time_count, height, LANES), F32),
-        in_specs=[ANY] * 5 + [VMEM] * 2,
+        in_specs=[ANY] * 9,
         out_specs=VMEM,
         scratch_shapes=[
             pltpu.VMEM((days_dev, 1, obs_dev), jnp.int32),
@@ -527,13 +559,17 @@
             pltpu.VMEM((days_dev, obs_dev), F32),
             pltpu.VMEM((days_dev, obs_dev), F32),
             pltpu.VMEM((members, cells), BF16),
+            pltpu.VMEM((rank, members), BF16),
+            pltpu.VMEM((1, members), F32),
+            pltpu.VMEM((days_dev, rank), F32),
+            pltpu.VMEM((1, days_dev), F32),
             pltpu.VMEM(slab, F32),
             pltpu.VMEM(slab, F32),
             pltpu.VMEM(((2 * days_dev + 1) * members + 16, 8 * LANES), BF16),
             pltpu.VMEM((days_dev, 4 * (cells // LANES), LANES), F32),
             pltpu.VMEM(part, F32),
             pltpu.VMEM(part, F32),
-            dma((5,)),
+            dma((9,)),
             dma((space_count,)),
             dma((space_count,)),
             dma((space_count,)),
@@ -554,7 +590,9 @@
         obs_weight,
         back,
         probe_rows,
-        extra,
+        scale_row,
+        decay,
+        inflation[None, :],
     )
     reach = 1 << ((days - 1).bit_length() - 1)
     return pl.pallas_call(
@@ -571,7 +609,7 @@
         ],
         compiler_params=PARAMS,
         name="smoother",
-    )(summed, probe_rows, member_scale[None, :], back)
+    )(summed, probe_rows, scale_row, back)
 
 
 def solution(mesh):

time: 110 us -> 59.6 us (0.54)
  Pallas kernels: 106 us -> 58.6 us
  local copies, waits for them, and re-layouts: 1.62 us -> 0 us
  other arithmetic: 1.29 us -> 0 us
    pallas_call x1, Pallas kernels: 74.4 us -> 27.9 us  [body(): pl.pallas_call(functools.partial(smooth_kernel, days_dev), out_shape=[jax...]
    unnamed x9 -> x0, local copies, waits for them, and re-layouts: 1.46 us -> none
where the time goes in v3:
time: 59.6 us; the launch traced here: 59.4 us
  Pallas kernels  58.6 us (98%)
  between operations  0.8 us (1%)
    pallas_call x1, Pallas kernels, body(): pl.pallas_call(functools.partial(gather_kernel, time_count, space_count,...  30.7 us
    pallas_call x1, Pallas kernels, body(): pl.pallas_call(functools.partial(smooth_kernel, days_dev), out_shape=[jax...  27.9 us

profile of v3, /device:TPU:0, one launch (start us, length us, event | category | flops | bytes accessed | tf_op | source)
XLA Modules:
  0.0 59.4 jit_solution(12256361281597548307)
XLA Ops:
  0.6 30.7 %gather.1.pay_ref = f32[8,4,8,128]{3,2,1,0:T(8,128)} custom-call(s32[3,1,2048]{2,1,0:T(1,128)} %bitcast.9, s32[3,2048]{1,0:T(4,128)} %offset_hbm.1, f32[3,2048]{1,0:T(4,128)} %value_hbm.1, f32[3,2048]{1,0:T(4,128)} %weight_hbm.1, bf16[64,8192]{1,0:T(8,128)(2,1)} %bitcast.5, bf16[32,64]{1,0:T(8,128)(2,1)} %bitcast.7, f32[1,64]{1,0:T(1,128)} %bitcast.10, ...), custom_call_target="tpu_custom_call" | custom-call | tf_op jit(solution)/shard_map/gather/pallas_call | solution.py:551
  31.3 27.9 %smoother.1 = (f32[3,8192]{1,0:T(4,128)}, f32[3,8192]{1,0:T(4,128)}) custom-call(f32[8,4,8,128]{3,2,1,0:T(8,128)} %gather.1.pay_ref, bf16[32,64]{1,0:T(8,128)(2,1)} %bitcast.8, f32[1,64]{1,0:T(1,128)} %bitcast.11, bf16[64,8192]{1,0:T(8,128)(2,1)} %bitcast.6), custom_call_target="tpu_custom_call" | custom-call | tf_op jit(solution)/shard_map/smoother/pallas_call | solution.py:598

commit v4 on v3

--- a/solution.py
+++ b/solution.py
@@ -480,9 +480,9 @@
     def stage(index, _):
         distance = jnp.left_shift(1, index)
         mats = [aug_ref[t] for t in range(days)]
-        solved = eliminate(mats, rank, False)
+        halves = [factor_rows(mat, rank, eye) for mat in eliminate(mats, rank, True)]
         for t in range(days):
-            product = dot_terms_tn(aug_ref[t], solved[t])
+            product = dot_terms_tn(halves[t], halves[t])
             top = product[:rank]
             low = product[2 * rank : 3 * rank]
             top_ref[reach + t] = jnp.where(

time: 59.6 us -> 60.7 us (1.018)
  Pallas kernels: 58.6 us -> 59.7 us
    pallas_call x1, Pallas kernels: 27.9 us -> 29 us  [body(): pl.pallas_call(functools.partial(smooth_kernel, days_dev), out_shape=[jax...]
where the time goes in v4:
time: 60.7 us; the launch traced here: 60.5 us
  Pallas kernels  59.7 us (98%)
  between operations  0.8 us (1%)
    pallas_call x1, Pallas kernels, body(): pl.pallas_call(functools.partial(gather_kernel, time_count, space_count,...  30.7 us
    pallas_call x1, Pallas kernels, body(): pl.pallas_call(functools.partial(smooth_kernel, days_dev), out_shape=[jax...  29 us

profile of v4, /device:TPU:0, one launch (start us, length us, event | category | flops | bytes accessed | tf_op | source)
XLA Modules:
  0.0 60.5 jit_solution(17964488443441729129)
XLA Ops:
  0.6 30.7 %gather.1.pay_ref = f32[8,4,8,128]{3,2,1,0:T(8,128)} custom-call(s32[3,1,2048]{2,1,0:T(1,128)} %bitcast.9, s32[3,2048]{1,0:T(4,128)} %offset_hbm.1, f32[3,2048]{1,0:T(4,128)} %value_hbm.1, f32[3,2048]{1,0:T(4,128)} %weight_hbm.1, bf16[64,8192]{1,0:T(8,128)(2,1)} %bitcast.5, bf16[32,64]{1,0:T(8,128)(2,1)} %bitcast.7, f32[1,64]{1,0:T(1,128)} %bitcast.10, ...), custom_call_target="tpu_custom_call" | custom-call | tf_op jit(solution)/shard_map/gather/pallas_call | solution.py:551
  31.3 29.0 %smoother.1 = (f32[3,8192]{1,0:T(4,128)}, f32[3,8192]{1,0:T(4,128)}) custom-call(f32[8,4,8,128]{3,2,1,0:T(8,128)} %gather.1.pay_ref, bf16[32,64]{1,0:T(8,128)(2,1)} %bitcast.8, f32[1,64]{1,0:T(1,128)} %bitcast.11, bf16[64,8192]{1,0:T(8,128)(2,1)} %bitcast.6), custom_call_target="tpu_custom_call" | custom-call | tf_op jit(solution)/shard_map/smoother/pallas_call | solution.py:598
